TPU v7x, 512 devices: a whole 4x8x8 slice. The times are simulated.
512 devices in a mesh: space: 32 (over z_lo, y, core), mode: 16 (over z_hi, x).
Axes of the slice: x: 4, y: 8, z: 8 (z_hi: 4, z_lo: 2; z = z_hi * 2 + z_lo), core: 2. Of those that a mesh axis runs over, the one named last changes fastest.
Arguments:
- occupation_deviation: float32 [2048, 64, 4, 128], P('mode', 'space'), may hold values from -6 to 6
- initial_thermal_offset: float32 [64, 4, 128], P('space'), may hold values from -6 to 6
- branch_specific_warmth: float32 [2048], replicated, may hold values from 0.2 to 2
- courant_numbers: float32 [3, 2048], P(None, 'mode'), may hold values from 0.02 to 0.3
- sign_quadrant: int32 [2048], P('mode'), may hold values from 0 to 7
- scattering_matrix: bfloat16 [2048, 2048], P('mode'), may hold values from -1 to 1
Outputs:
- population_out: float32 [2048, 64, 4, 128], P('mode', 'space')
- thermal_offset: float32 [64, 4, 128], P('space')
All inputs are finite; a program needn't handle non-finite values.
Results may differ from a plain program's by a relative error of at most 0.002.
Values may be sent and summed in bfloat16 or wider, within the bound.
A program may use at most 64 MiB of HBM per device.

v0:
```python
import jax
import jax.numpy as jnp
from jax import lax
from jax.sharding import PartitionSpec as P

ITERS = 3


def padded_2(cells, sides, width):
    for axis, dim in sides:
        count = lax.axis_size(axis)
        head = lax.slice_in_dim(cells, 0, width, axis=dim)
        tail = lax.slice_in_dim(cells, cells.shape[dim] - width, cells.shape[dim], axis=dim)
        cells = jnp.concatenate(
            [
                lax.ppermute(tail, axis, [(i, (i + 1) % count) for i in range(count)]),
                cells,
                lax.ppermute(head, axis, [((i + 1) % count, i) for i in range(count)]),
            ],
            axis=dim,
        )
    return cells


def copy_for_each(x, axis):
    length = lax.axis_size(axis)
    return lax.all_to_all(jnp.broadcast_to(x[None], (length, *x.shape)), axis, 0, 0, tiled=True)


def joined_along(blocks, dim):
    shape = list(blocks.shape[1:])
    shape[dim] *= blocks.shape[0]
    return jnp.moveaxis(blocks, 0, dim).reshape(shape)


def gather_directly(x, axis, dim):
    blocks = copy_for_each(x, axis)
    return joined_along(blocks, dim)


def advect(lattice_wave_carry, courant_numbers, sign_quadrant):
    padded = padded_2(lattice_wave_carry, (("space", 1),), 1)
    advected = lattice_wave_carry
    for dim_index in range(3):
        if dim_index == 0:
            below_side = padded[:, :-2]
            above_side = padded[:, 2:]
        else:
            below_side = jnp.roll(lattice_wave_carry, 1, dim_index + 1)
            above_side = jnp.roll(lattice_wave_carry, -1, dim_index + 1)
        sign_bit = (sign_quadrant >> dim_index & 1).reshape(-1, 1, 1, 1)
        upwind = jnp.where(sign_bit == 1, above_side, below_side)
        advected = advected - courant_numbers[dim_index].reshape(-1, 1, 1, 1) * (
            lattice_wave_carry - upwind
        )
    return advected


def shards(
    occupation_deviation,
    initial_thermal_offset,
    branch_specific_warmth,
    courant_numbers,
    sign_quadrant,
    scattering_matrix,
):
    local_modes = occupation_deviation.shape[0]
    partition_extents = occupation_deviation.shape
    cell_count = partition_extents[1] * partition_extents[2] * partition_extents[3]
    first_mode = lax.axis_index("mode") * local_modes
    device_specific_warmth = lax.dynamic_slice_in_dim(
        branch_specific_warmth, first_mode, local_modes
    )
    summed_specific_warmth = jnp.sum(branch_specific_warmth)
    lattice_wave_carry = (
        occupation_deviation
        + device_specific_warmth.reshape(-1, 1, 1, 1) * initial_thermal_offset[None]
    )
    scattering_stripes = jnp.dot(
        scattering_matrix.astype(jnp.float32),
        branch_specific_warmth,
        precision=lax.Precision.HIGHEST,
    )
    full_matrix = lax.all_gather(scattering_matrix, "mode", axis=0, tiled=True)
    thermal_offset = jnp.zeros(partition_extents[1:], jnp.float32)
    for iteration in range(ITERS):
        upstream_occupation = advect(lattice_wave_carry, courant_numbers, sign_quadrant)
        moved_bf = upstream_occupation.astype(jnp.bfloat16)
        local_flat_bf = moved_bf.reshape(local_modes, cell_count)
        all_modes = lax.all_to_all(local_flat_bf, "mode", split_axis=1, concat_axis=0, tiled=True)
        block_product = jnp.dot(full_matrix, all_modes, preferred_element_type=jnp.float32)
        block_energy = jnp.dot(
            branch_specific_warmth, all_modes.astype(jnp.float32), precision=lax.Precision.HIGHEST
        )
        scattering_applied = lax.all_to_all(
            block_product, "mode", split_axis=0, concat_axis=1, tiled=True
        )
        internal_warmth_field = gather_directly(block_energy, "mode", 0)
        thermal_offset = (internal_warmth_field / summed_specific_warmth).reshape(
            partition_extents[1:]
        )
        lattice_wave_carry = (
            upstream_occupation
            - scattering_applied.reshape(partition_extents)
            + scattering_stripes.reshape(-1, 1, 1, 1) * thermal_offset[None]
        )
    return (lattice_wave_carry, thermal_offset)


def solution(mesh):
    placed = (
        P("mode", "space", None, None),
        P("space", None, None),
        P(),
        P(None, "mode"),
        P("mode"),
        P("mode", None),
    )
    return jax.shard_map(
        shards,
        mesh=mesh,
        in_specs=placed,
        out_specs=(P("mode", "space", None, None), P("space", None, None)),
        check_vma=False,
    )
```

profile of v0, /device:TPU:16, one launch (start us, length us, event | category | flops | bytes accessed | tf_op | source)
XLA Modules:
  0.0 312.7 jit_solution(900750973917751772)
XLA Ops:
  7.2 0.7 all-gather.2.cloned.1.call-update
  7.9 1.2 copy.19
  9.2 0.8 dynamic_slice.3
  9.9 0.9 multiply_add_fusion.3
  10.9 1.9 collective-permute-start
  12.8 2.4 collective-permute-start.1
  15.2 0.7 and_compare_fusion.2
  15.9 0.8 slice_bitcast_fusion.2
  16.8 0.1 fusion.61
  16.9 3.6 %collective-permute-done.1 = f32[128,1,4,128]{0,3,2,1:T(8,128)S(1)} collective-permute-done((f32[128,1,4,128]{0,3,2,1:T(8,128)S(1)}, f32[128,1,4,128]{0,3,2,1:T(8,128)S(1)}, u32[]{:S(2)}, u32[]{:S(2)}) %collective-permute-start.1) | collective-permute-done | bytes 262176 | tf_op jit(solution)/shard_map/ppermute | solution.py:16
  20.5 0.3 fusion.46
  20.8 30.4 %all_to_all.123 = bf16[128,16,64]{0,2,1:T(8,128)(2,1)S(1)} all-to-all(bf16[128,16,64]{0,2,1:T(8,128)(2,1)S(1)} %bitcast.99), channel_id=1, replica_groups=mesh['space'=32,'mode'=16] {'mode'}, dimensions={1} | all-to-all | bytes 524288 | tf_op jit(solution)/shard_map/all_to_all | solution.py:90
  51.2 0.3 convolution_bitcast_fusion.5
  51.5 0.6 broadcast_in_dim.58
  52.1 6.0 %all-to-all-start.2 = ((f32[16,1,64]{2,1,0:T(1,128)}), f32[16,1,64]{2,1,0:T(1,128)S(1)}, u32[]{:S(2)}, u32[]{:S(2)}) async-start(f32[16,1,64]{2,1,0:T(1,128)} %broadcast_in_dim.58), calls=%async_computation.2 | async-start | bytes 16384 | tf_op jit(solution)/shard_map/all_to_all | solution.py:27
  58.1 86.2 %all-gather.2.cloned.1.call-done = bf16[2048,2048]{1,0:T(8,128)(2,1)} async-done(((bf16[128,2048]{1,0:T(8,128)(2,1)}), bf16[2048,2048]{1,0:T(8,128)(2,1)}) %all-gather.2.cloned.1.call-update) | async-done | bytes 8388624 | tf_op jit(solution)/shard_map/all_gather | solution.py:84
  144.3 6.0 %convolution_bitcast_fusion.2 = f32[8,16,8,128]{3,2,1,0:T(8,128)S(1)} fusion(bf16[2048,2048]{1,0:T(8,128)(2,1)} %all-gather.2.cloned.1.call-done, bf16[128,16,64]{0,2,1:T(8,128)(2,1)S(1)} %all_to_all.123), kind=kOutput, calls=%fused_computation.2 | convolution fusion | flops 536870912 | bytes 9175040 | tf_op jit(solution)/shard_map/dot_general | solution.py:91
  150.3 0.9 copy.62
  151.2 6.2 %all-to-all-start.1 = ((f32[16,128,64]{1,2,0:T(8,128)}), f32[16,128,64]{1,2,0:T(8,128)S(1)}, u32[]{:S(2)}, u32[]{:S(2)}) async-start(f32[16,128,64]{1,2,0:T(8,128)} %bitcast.94), calls=%async_computation.1 | async-start | bytes 1048576 | tf_op jit(solution)/shard_map/all_to_all | solution.py:95
  157.4 0.6 reduce_sum.9
  158.0 0.5 convolution_bitcast_fusion.6
  158.5 0.7 divide_reduce_fusion.2
  159.2 0.1 div.38
  159.3 15.9 %all-to-all-done.1 = f32[16,128,64]{1,2,0:T(8,128)S(1)} async-done(((f32[16,128,64]{1,2,0:T(8,128)}), f32[16,128,64]{1,2,0:T(8,128)S(1)}, u32[]{:S(2)}, u32[]{:S(2)}) %all-to-all-start.1) | async-done | bytes 524320 | tf_op jit(solution)/shard_map/all_to_all | solution.py:95
  175.1 0.2 multiply_add_fusion.2
  175.5 0.1 fusion.54
  175.5 1.9 collective-permute-start.2
  177.5 2.4 collective-permute-start.3
  179.9 0.1 fusion.56
  180.0 1.4 collective-permute-done.2
  181.3 3.8 %collective-permute-done.3 = f32[128,1,4,128]{0,3,2,1:T(8,128)S(1)} collective-permute-done((f32[128,1,4,128]{0,3,2,1:T(8,128)S(1)}, f32[128,1,4,128]{0,3,2,1:T(8,128)S(1)}, u32[]{:S(2)}, u32[]{:S(2)}) %collective-permute-start.3) | collective-permute-done | bytes 262176 | tf_op jit(solution)/shard_map/ppermute | solution.py:16
  185.1 0.3 fusion.44
  185.5 16.2 %all_to_all.124 = bf16[128,16,64]{0,2,1:T(8,128)(2,1)S(1)} all-to-all(bf16[128,16,64]{0,2,1:T(8,128)(2,1)S(1)} %bitcast.100), channel_id=1, replica_groups=mesh['space'=32,'mode'=16] {'mode'}, dimensions={1} | all-to-all | bytes 524288 | tf_op jit(solution)/shard_map/all_to_all | solution.py:90
  201.7 0.3 convolution_bitcast_fusion.4
  202.0 0.6 broadcast_in_dim.59
  202.6 3.8 %all-to-all-start.5 = ((f32[16,1,64]{2,1,0:T(1,128)}), f32[16,1,64]{2,1,0:T(1,128)S(1)}, u32[]{:S(2)}, u32[]{:S(2)}) async-start(f32[16,1,64]{2,1,0:T(1,128)} %broadcast_in_dim.59), calls=%async_computation.5 | async-start | bytes 16384 | tf_op jit(solution)/shard_map/all_to_all | solution.py:27
  206.4 6.0 %convolution_bitcast_fusion.1 = f32[8,16,8,128]{3,2,1,0:T(8,128)S(1)} fusion(bf16[2048,2048]{1,0:T(8,128)(2,1)} %all-gather.2.cloned.1.call-done, bf16[128,16,64]{0,2,1:T(8,128)(2,1)S(1)} %all_to_all.124), kind=kOutput, calls=%fused_computation.1 | convolution fusion | flops 536870912 | bytes 9175040 | tf_op jit(solution)/shard_map/dot_general | solution.py:91
  212.4 0.9 copy.61
  213.3 2.9 all-to-all-done.5
  216.2 6.7 %all-to-all-start.4 = ((f32[16,128,64]{1,2,0:T(8,128)}), f32[16,128,64]{1,2,0:T(8,128)S(1)}, u32[]{:S(2)}, u32[]{:S(2)}) async-start(f32[16,128,64]{1,2,0:T(8,128)} %bitcast.93), calls=%async_computation.4 | async-start | bytes 1048576 | tf_op jit(solution)/shard_map/all_to_all | solution.py:95
  222.9 0.7 divide_reduce_fusion.1
  223.6 0.1 div.40
  223.6 14.6 %all-to-all-done.4 = f32[16,128,64]{1,2,0:T(8,128)S(1)} async-done(((f32[16,128,64]{1,2,0:T(8,128)}), f32[16,128,64]{1,2,0:T(8,128)S(1)}, u32[]{:S(2)}, u32[]{:S(2)}) %all-to-all-start.4) | async-done | bytes 524320 | tf_op jit(solution)/shard_map/all_to_all | solution.py:95
  238.3 0.2 multiply_add_fusion.1
  238.6 0.1 fusion.49
  238.7 1.9 collective-permute-start.4
  240.6 2.4 collective-permute-start.5
  243.0 0.1 fusion.51
  243.1 1.4 collective-permute-done.4
  244.5 3.8 %collective-permute-done.5 = f32[128,1,4,128]{0,3,2,1:T(8,128)S(1)} collective-permute-done((f32[128,1,4,128]{0,3,2,1:T(8,128)S(1)}, f32[128,1,4,128]{0,3,2,1:T(8,128)S(1)}, u32[]{:S(2)}, u32[]{:S(2)}) %collective-permute-start.5) | collective-permute-done | bytes 262176 | tf_op jit(solution)/shard_map/ppermute | solution.py:16
  248.3 0.3 fusion.42
  248.6 17.0 %all_to_all.125 = bf16[128,16,64]{0,2,1:T(8,128)(2,1)S(1)} all-to-all(bf16[128,16,64]{0,2,1:T(8,128)(2,1)S(1)} %bitcast.98), channel_id=1, replica_groups=mesh['space'=32,'mode'=16] {'mode'}, dimensions={1} | all-to-all | bytes 524288 | tf_op jit(solution)/shard_map/all_to_all | solution.py:90
  265.6 0.3 convolution_bitcast_fusion.3
  265.9 0.6 broadcast_in_dim.60
  266.5 4.6 %all-to-all-start.8 = ((f32[16,1,64]{2,1,0:T(1,128)}), f32[16,1,64]{2,1,0:T(1,128)S(1)}, u32[]{:S(2)}, u32[]{:S(2)}) async-start(f32[16,1,64]{2,1,0:T(1,128)} %broadcast_in_dim.60), calls=%async_computation.8 | async-start | bytes 16384 | tf_op jit(solution)/shard_map/all_to_all | solution.py:27
  271.2 6.0 %convolution_bitcast_fusion = f32[8,16,8,128]{3,2,1,0:T(8,128)S(1)} fusion(bf16[2048,2048]{1,0:T(8,128)(2,1)} %all-gather.2.cloned.1.call-done, bf16[128,16,64]{0,2,1:T(8,128)(2,1)S(1)} %all_to_all.125), kind=kOutput, calls=%fused_computation | convolution fusion | flops 536870912 | bytes 9175040 | tf_op jit(solution)/shard_map/dot_general | solution.py:91
  277.2 0.9 copy.60
  278.1 2.9 all-to-all-done.8
  281.0 6.7 %all-to-all-start.7 = ((f32[16,128,64]{1,2,0:T(8,128)}), f32[16,128,64]{1,2,0:T(8,128)S(1)}, u32[]{:S(2)}, u32[]{:S(2)}) async-start(f32[16,128,64]{1,2,0:T(8,128)} %bitcast.92), calls=%async_computation.7 | async-start | bytes 1048576 | tf_op jit(solution)/shard_map/all_to_all | solution.py:95
  287.7 0.7 divide_reduce_fusion
  288.4 0.1 div.42
  288.5 16.2 %all-to-all-done.7 = f32[16,128,64]{1,2,0:T(8,128)S(1)} async-done(((f32[16,128,64]{1,2,0:T(8,128)}), f32[16,128,64]{1,2,0:T(8,128)S(1)}, u32[]{:S(2)}, u32[]{:S(2)}) %all-to-all-start.7) | async-done | bytes 524320 | tf_op jit(solution)/shard_map/all_to_all | solution.py:95
  304.6 0.2 multiply_add_fusion
  304.9 1.0 copy.26
  (19 shorter events, 0.3 us)
Async XLA Ops:
  7.2 44.0 %copy-start.1 = (f32[2048]{0:T(1024)S(1)}, f32[2048]{0:T(1024)}, u32[]{:S(2)}) copy-start(f32[2048]{0:T(1024)} %param.8) | copy-start | bytes 24580
  7.2 137.1 %all-gather.2.cloned.1.call-start = ((), (), s32[]{:S(2)}) async-start(), calls=%async_computation.9 | async-start | bytes 8912896 | tf_op jit(solution)/shard_map/all_gather | solution.py:84
  10.9 6.0 %collective-permute-start = (f32[128,1,4,128]{0,3,2,1:T(8,128)S(1)}, f32[128,1,4,128]{0,3,2,1:T(8,128)S(1)}, u32[]{:S(2)}, u32[]{:S(2)}) collective-permute-start(f32[128,1,4,128]{0,3,2,1:T(8,128)S(1)} %get-tuple-element.32), channel_id=1, source_target_pairs={{16,0},{32,16},{48,32},{64,48},{80,64},{96,80},{112,96},{128,112},... | collective-permute-start | bytes 786440 | tf_op jit(solution)/shard_map/ppermute | solution.py:18
  12.8 7.7 %collective-permute-start.1 = (f32[128,1,4,128]{0,3,2,1:T(8,128)S(1)}, f32[128,1,4,128]{0,3,2,1:T(8,128)S(1)}, u32[]{:S(2)}, u32[]{:S(2)}) collective-permute-start(f32[128,1,4,128]{0,3,2,1:T(8,128)S(1)} %get-tuple-element.33), channel_id=1, source_target_pairs={{0,16},{16,32},{32,48},{48,64},{64,80},{80,96},{96,112},{112,128},... | collective-permute-start | bytes 786440 | tf_op jit(solution)/shard_map/ppermute | solution.py:16
  16.9 141.1 %copy-start = (bf16[128,2048]{1,0:T(8,128)(2,1)S(1)}, bf16[128,2048]{1,0:T(8,128)(2,1)}, u32[]{:S(2)}) copy-start(bf16[128,2048]{1,0:T(8,128)(2,1)} %param.11) | copy-start | bytes 1572868
  52.1 99.1 %all-to-all-start.2 = ((f32[16,1,64]{2,1,0:T(1,128)}), f32[16,1,64]{2,1,0:T(1,128)S(1)}, u32[]{:S(2)}, u32[]{:S(2)}) async-start(f32[16,1,64]{2,1,0:T(1,128)} %broadcast_in_dim.58), calls=%async_computation.2 | async-start | bytes 16384 | tf_op jit(solution)/shard_map/all_to_all | solution.py:27
  151.2 23.9 %all-to-all-start.1 = ((f32[16,128,64]{1,2,0:T(8,128)}), f32[16,128,64]{1,2,0:T(8,128)S(1)}, u32[]{:S(2)}, u32[]{:S(2)}) async-start(f32[16,128,64]{1,2,0:T(8,128)} %bitcast.94), calls=%async_computation.1 | async-start | bytes 1048576 | tf_op jit(solution)/shard_map/all_to_all | solution.py:95
  175.5 5.8 %collective-permute-start.2 = (f32[128,1,4,128]{0,3,2,1:T(8,128)S(1)}, f32[128,1,4,128]{0,3,2,1:T(8,128)S(1)}, u32[]{:S(2)}, u32[]{:S(2)}) collective-permute-start(f32[128,1,4,128]{0,3,2,1:T(8,128)S(1)} %get-tuple-element.22), channel_id=1, source_target_pairs={{16,0},{32,16},{48,32},{64,48},{80,64},{96,80},{112,96},{128,112},... | collective-permute-start | bytes 786440 | tf_op jit(solution)/shard_map/ppermute | solution.py:18
  177.5 7.7 %collective-permute-start.3 = (f32[128,1,4,128]{0,3,2,1:T(8,128)S(1)}, f32[128,1,4,128]{0,3,2,1:T(8,128)S(1)}, u32[]{:S(2)}, u32[]{:S(2)}) collective-permute-start(f32[128,1,4,128]{0,3,2,1:T(8,128)S(1)} %get-tuple-element.23), channel_id=1, source_target_pairs={{0,16},{16,32},{32,48},{48,64},{64,80},{80,96},{96,112},{112,128},... | collective-permute-start | bytes 786440 | tf_op jit(solution)/shard_map/ppermute | solution.py:16
  202.6 13.6 %all-to-all-start.5 = ((f32[16,1,64]{2,1,0:T(1,128)}), f32[16,1,64]{2,1,0:T(1,128)S(1)}, u32[]{:S(2)}, u32[]{:S(2)}) async-start(f32[16,1,64]{2,1,0:T(1,128)} %broadcast_in_dim.59), calls=%async_computation.5 | async-start | bytes 16384 | tf_op jit(solution)/shard_map/all_to_all | solution.py:27
  216.2 22.1 %all-to-all-start.4 = ((f32[16,128,64]{1,2,0:T(8,128)}), f32[16,128,64]{1,2,0:T(8,128)S(1)}, u32[]{:S(2)}, u32[]{:S(2)}) async-start(f32[16,128,64]{1,2,0:T(8,128)} %bitcast.93), calls=%async_computation.4 | async-start | bytes 1048576 | tf_op jit(solution)/shard_map/all_to_all | solution.py:95
  238.7 5.8 %collective-permute-start.4 = (f32[128,1,4,128]{0,3,2,1:T(8,128)S(1)}, f32[128,1,4,128]{0,3,2,1:T(8,128)S(1)}, u32[]{:S(2)}, u32[]{:S(2)}) collective-permute-start(f32[128,1,4,128]{0,3,2,1:T(8,128)S(1)} %get-tuple-element.12), channel_id=1, source_target_pairs={{16,0},{32,16},{48,32},{64,48},{80,64},{96,80},{112,96},{128,112},... | collective-permute-start | bytes 786440 | tf_op jit(solution)/shard_map/ppermute | solution.py:18
  240.6 7.7 %collective-permute-start.5 = (f32[128,1,4,128]{0,3,2,1:T(8,128)S(1)}, f32[128,1,4,128]{0,3,2,1:T(8,128)S(1)}, u32[]{:S(2)}, u32[]{:S(2)}) collective-permute-start(f32[128,1,4,128]{0,3,2,1:T(8,128)S(1)} %get-tuple-element.13), channel_id=1, source_target_pairs={{0,16},{16,32},{32,48},{48,64},{64,80},{80,96},{96,112},{112,128},... | collective-permute-start | bytes 786440 | tf_op jit(solution)/shard_map/ppermute | solution.py:16
  266.5 14.5 %all-to-all-start.8 = ((f32[16,1,64]{2,1,0:T(1,128)}), f32[16,1,64]{2,1,0:T(1,128)S(1)}, u32[]{:S(2)}, u32[]{:S(2)}) async-start(f32[16,1,64]{2,1,0:T(1,128)} %broadcast_in_dim.60), calls=%async_computation.8 | async-start | bytes 16384 | tf_op jit(solution)/shard_map/all_to_all | solution.py:27
  281.0 23.6 %all-to-all-start.7 = ((f32[16,128,64]{1,2,0:T(8,128)}), f32[16,128,64]{1,2,0:T(8,128)S(1)}, u32[]{:S(2)}, u32[]{:S(2)}) async-start(f32[16,128,64]{1,2,0:T(8,128)} %bitcast.92), calls=%async_computation.7 | async-start | bytes 1048576 | tf_op jit(solution)/shard_map/all_to_all | solution.py:95
  288.5 17.4 %copy-start.2 = (f32[2,4,128]{2,1,0:T(4,128)}, f32[2,4,128]{2,1,0:T(4,128)S(1)}, u32[]{:S(2)}) copy-start(f32[2,4,128]{2,1,0:T(4,128)S(1)} %div.42) | copy-start | bytes 12292
Sparse Core Ops, SparseCore 0:
  11.0 133.2 all-gather.1
where the time goes:
time: 314 us; the launch traced here: 313 us
  waiting for transfers between devices  153 us (49%)
  blocking collectives  63.5 us (20%)
  starting transfers between devices  47 us (15%)
  matrix products  19.5 us (6%)
  between operations  14.3 us (5%)
  local copies, waits for them, and re-layouts  9.09 us (3%)
  other arithmetic  5.87 us (2%)
    all_gather x1, waiting for transfers between devices, shards(): full_matrix = lax.all_gather(scattering_matrix, 'mode', axis=0, tiled=True)  86.2 us
    all_to_all x3, blocking collectives, shards(): lax.all_to_all(local_flat_bf, 'mode', split_axis=1, concat_axis=0, tiled=...  63.5 us
    all_to_all x3, waiting for transfers between devices, shards(): lax.all_to_all(block_product, 'mode', split_axis=0, concat_axis=1, tiled=...  46.7 us
    all_to_all x3, starting transfers between devices, shards(): lax.all_to_all(block_product, 'mode', split_axis=0, concat_axis=1, tiled=...  19.6 us
    dot_general x3, matrix products, shards(): jnp.dot(full_matrix, all_modes, preferred_element_type=jnp.float32)  18.1 us
    all_to_all x3, starting transfers between devices, copy_for_each(): lax.all_to_all(jnp.broadcast_to(x[None], (length, *x.shape)), axis, 0, 0,...  14.4 us
    ppermute x3, waiting for transfers between devices, padded_2(): lax.ppermute(tail, axis, [(i, (i + 1) % count) for i in range(count)])  11.2 us
    ppermute x3, starting transfers between devices, padded_2(): lax.ppermute(tail, axis, [(i, (i + 1) % count) for i in range(count)])  7.22 us
  transfers between devices with their start and end apart: 13, of which 11 were waited for; matrix products, arithmetic and copies ran while one was open for 10% of the time, Pallas kernels for 0%

commit v1 on v0

--- a/solution.py
+++ b/solution.py
@@ -81,7 +81,9 @@
         branch_specific_warmth,
         precision=lax.Precision.HIGHEST,
     )
-    full_matrix = lax.all_gather(scattering_matrix, "mode", axis=0, tiled=True)
+    full_matrix = jnp.concatenate(
+        lax.all_to_all(jnp.stack([scattering_matrix] * lax.axis_size("mode")), "mode", 0, 0), axis=0
+    )
     thermal_offset = jnp.zeros(partition_extents[1:], jnp.float32)
     for iteration in range(ITERS):
         upstream_occupation = advect(lattice_wave_carry, courant_numbers, sign_quadrant)

time: 314 us -> 414 us (1.32)
  the two profiles are of different devices: /device:TPU:16 before, /device:TPU:4 now
where the time goes in v1:
time: 414 us; the launch traced here: 412 us
  waiting for transfers between devices  239 us (58%)
  starting transfers between devices  77.8 us (19%)
  blocking collectives  55.7 us (13%)
  matrix products  19.5 us (5%)
  local copies, waits for them, and re-layouts  13.4 us (3%)
  other arithmetic  5.85 us (1%)
    all_to_all x1, waiting for transfers between devices, shards(): lax.all_to_all(jnp.stack([scattering_matrix] * lax.axis_size('mode')), 'm...  184 us
    all_to_all x3, blocking collectives, shards(): lax.all_to_all(local_flat_bf, 'mode', split_axis=1, concat_axis=0, tiled=...  55.7 us
    all_to_all x3, waiting for transfers between devices, shards(): lax.all_to_all(block_product, 'mode', split_axis=0, concat_axis=1, tiled=...  30.2 us
    all_to_all x3, starting transfers between devices, shards(): lax.all_to_all(block_product, 'mode', split_axis=0, concat_axis=1, tiled=...  26.3 us
    ppermute x3, starting transfers between devices, padded_2(): lax.ppermute(head, axis, [((i + 1) % count, i) for i in range(count)])  21.1 us
    ppermute x3, waiting for transfers between devices, padded_2(): lax.ppermute(tail, axis, [(i, (i + 1) % count) for i in range(count)])  18.5 us
    dot_general x3, matrix products, shards(): jnp.dot(full_matrix, all_modes, preferred_element_type=jnp.float32)  18.1 us
    all_to_all x3, starting transfers between devices, copy_for_each(): lax.all_to_all(jnp.broadcast_to(x[None], (length, *x.shape)), axis, 0, 0,...  17.6 us
  transfers between devices with their start and end apart: 13, of which 13 were waited for; matrix products, arithmetic and copies ran while one was open for 6% of the time, Pallas kernels for 0%

profile of v1, /device:TPU:4, one launch (start us, length us, event | category | flops | bytes accessed | tf_op | source)
XLA Modules:
  0.0 412.4 jit_solution(14406199927744618353)
XLA Ops:
  0.6 1.3 copy.19
  1.9 0.8 dynamic_slice.3
  2.7 0.9 multiply_add_fusion.3
  3.6 6.6 %collective-permute-start = (f32[128,1,4,128]{0,3,2,1:T(8,128)S(1)}, f32[128,1,4,128]{0,3,2,1:T(8,128)S(1)}, u32[]{:S(2)}, u32[]{:S(2)}) collective-permute-start(f32[128,1,4,128]{0,3,2,1:T(8,128)S(1)} %get-tuple-element.32), channel_id=1, source_target_pairs={{16,0},{32,16},{48,32},{64,48},{80,64},{96,80},{112,96},{128,112},... | collective-permute-start | bytes 786440 | tf_op jit(solution)/shard_map/ppermute | solution.py:18
  10.3 1.9 collective-permute-start.1
  12.3 0.8 slice_bitcast_fusion.2
  13.1 0.7 and_compare_fusion.2
  13.8 0.1 fusion.61
  13.9 0.3 collective-permute-done
  14.1 5.9 %collective-permute-done.1 = f32[128,1,4,128]{0,3,2,1:T(8,128)S(1)} collective-permute-done((f32[128,1,4,128]{0,3,2,1:T(8,128)S(1)}, f32[128,1,4,128]{0,3,2,1:T(8,128)S(1)}, u32[]{:S(2)}, u32[]{:S(2)}) %collective-permute-start.1) | collective-permute-done | bytes 262176 | tf_op jit(solution)/shard_map/ppermute | solution.py:16
  20.1 0.3 fusion.46
  20.4 21.5 %all_to_all.128 = bf16[128,16,64]{0,2,1:T(8,128)(2,1)S(1)} all-to-all(bf16[128,16,64]{0,2,1:T(8,128)(2,1)S(1)} %bitcast.100), channel_id=1, replica_groups=mesh['space'=32,'mode'=16] {'mode'}, dimensions={1} | all-to-all | bytes 524288 | tf_op jit(solution)/shard_map/all_to_all | solution.py:92
  41.9 4.3 %stack.2 = bf16[16,128,2048]{2,1,0:T(8,128)(2,1)} broadcast(bf16[128,2048]{1,0:T(8,128)(2,1)S(1)} %copy-done), dimensions={1,2} | broadcast | bytes 8912896 | tf_op jit(solution)/shard_map/stack | solution.py:85
  46.2 6.5 %all-to-all-start.1 = ((bf16[16,128,2048]{2,1,0:T(8,128)(2,1)}), bf16[16,128,2048]{2,1,0:T(8,128)(2,1)}, u32[]{:S(2)}, u32[]{:S(2)}) async-start(bf16[16,128,2048]{2,1,0:T(8,128)(2,1)} %stack.2), calls=%async_computation.1 | async-start | bytes 16777216 | tf_op jit(solution)/shard_map/all_to_all | solution.py:85
  52.7 0.3 convolution_bitcast_fusion.5
  53.0 184.5 %all-to-all-done.1 = bf16[16,128,2048]{2,1,0:T(8,128)(2,1)} async-done(((bf16[16,128,2048]{2,1,0:T(8,128)(2,1)}), bf16[16,128,2048]{2,1,0:T(8,128)(2,1)}, u32[]{:S(2)}, u32[]{:S(2)}) %all-to-all-start.1) | async-done | bytes 8388640 | tf_op jit(solution)/shard_map/all_to_all | solution.py:85
  237.5 0.6 broadcast_in_dim.58
  238.1 7.1 %all-to-all-start.3 = ((f32[16,1,64]{2,1,0:T(1,128)}), f32[16,1,64]{2,1,0:T(1,128)S(1)}, u32[]{:S(2)}, u32[]{:S(2)}) async-start(f32[16,1,64]{2,1,0:T(1,128)} %broadcast_in_dim.58), calls=%async_computation.3 | async-start | bytes 16384 | tf_op jit(solution)/shard_map/all_to_all | solution.py:27
  245.2 6.0 %convolution_bitcast_fusion.2 = f32[8,16,8,128]{3,2,1,0:T(8,128)S(1)} fusion(bf16[2048,2048]{1,0:T(8,128)(2,1)} %bitcast.5, bf16[128,16,64]{0,2,1:T(8,128)(2,1)S(1)} %all_to_all.128), kind=kOutput, calls=%fused_computation.2 | convolution fusion | flops 536870912 | bytes 9175040 | tf_op jit(solution)/shard_map/dot_general | solution.py:93
  251.2 0.9 copy.62
  252.0 0.9 all-to-all-done.3
  252.9 8.8 %all-to-all-start.2 = ((f32[16,128,64]{1,2,0:T(8,128)}), f32[16,128,64]{1,2,0:T(8,128)S(1)}, u32[]{:S(2)}, u32[]{:S(2)}) async-start(f32[16,128,64]{1,2,0:T(8,128)} %bitcast.95), calls=%async_computation.2 | async-start | bytes 1048576 | tf_op jit(solution)/shard_map/all_to_all | solution.py:97
  261.7 0.6 reduce_sum.9
  262.3 0.5 convolution_bitcast_fusion.6
  262.8 0.7 divide_reduce_fusion.2
  263.6 9.8 %all-to-all-done.2 = f32[16,128,64]{1,2,0:T(8,128)S(1)} async-done(((f32[16,128,64]{1,2,0:T(8,128)}), f32[16,128,64]{1,2,0:T(8,128)S(1)}, u32[]{:S(2)}, u32[]{:S(2)}) %all-to-all-start.2) | async-done | bytes 524320 | tf_op jit(solution)/shard_map/all_to_all | solution.py:97
  273.4 0.2 multiply_add_fusion.2
  273.8 12.5 %collective-permute-start.2 = (f32[128,1,4,128]{0,3,2,1:T(8,128)S(1)}, f32[128,1,4,128]{0,3,2,1:T(8,128)S(1)}, u32[]{:S(2)}, u32[]{:S(2)}) collective-permute-start(f32[128,1,4,128]{0,3,2,1:T(8,128)S(1)} %get-tuple-element.22), channel_id=1, source_target_pairs={{16,0},{32,16},{48,32},{64,48},{80,64},{96,80},{112,96},{128,112},... | collective-permute-start | bytes 786440 | tf_op jit(solution)/shard_map/ppermute | solution.py:18
  286.3 1.9 collective-permute-start.3
  288.2 0.1 fusion.56
  288.3 1.9 collective-permute-done.2
  290.2 6.6 %collective-permute-done.3 = f32[128,1,4,128]{0,3,2,1:T(8,128)S(1)} collective-permute-done((f32[128,1,4,128]{0,3,2,1:T(8,128)S(1)}, f32[128,1,4,128]{0,3,2,1:T(8,128)S(1)}, u32[]{:S(2)}, u32[]{:S(2)}) %collective-permute-start.3) | collective-permute-done | bytes 262176 | tf_op jit(solution)/shard_map/ppermute | solution.py:16
  296.8 0.3 fusion.44
  297.1 18.4 %all_to_all.129 = bf16[128,16,64]{0,2,1:T(8,128)(2,1)S(1)} all-to-all(bf16[128,16,64]{0,2,1:T(8,128)(2,1)S(1)} %bitcast.101), channel_id=1, replica_groups=mesh['space'=32,'mode'=16] {'mode'}, dimensions={1} | all-to-all | bytes 524288 | tf_op jit(solution)/shard_map/all_to_all | solution.py:92
  315.5 0.3 convolution_bitcast_fusion.4
  315.8 0.6 broadcast_in_dim.59
  316.5 5.3 %all-to-all-start.6 = ((f32[16,1,64]{2,1,0:T(1,128)}), f32[16,1,64]{2,1,0:T(1,128)S(1)}, u32[]{:S(2)}, u32[]{:S(2)}) async-start(f32[16,1,64]{2,1,0:T(1,128)} %broadcast_in_dim.59), calls=%async_computation.6 | async-start | bytes 16384 | tf_op jit(solution)/shard_map/all_to_all | solution.py:27
  321.7 6.0 %convolution_bitcast_fusion.1 = f32[8,16,8,128]{3,2,1,0:T(8,128)S(1)} fusion(bf16[2048,2048]{1,0:T(8,128)(2,1)} %bitcast.5, bf16[128,16,64]{0,2,1:T(8,128)(2,1)S(1)} %all_to_all.129), kind=kOutput, calls=%fused_computation.1 | convolution fusion | flops 536870912 | bytes 9175040 | tf_op jit(solution)/shard_map/dot_general | solution.py:93
  327.8 0.9 copy.61
  328.6 0.8 all-to-all-done.6
  329.5 8.8 %all-to-all-start.5 = ((f32[16,128,64]{1,2,0:T(8,128)}), f32[16,128,64]{1,2,0:T(8,128)S(1)}, u32[]{:S(2)}, u32[]{:S(2)}) async-start(f32[16,128,64]{1,2,0:T(8,128)} %bitcast.94), calls=%async_computation.5 | async-start | bytes 1048576 | tf_op jit(solution)/shard_map/all_to_all | solution.py:97
  338.3 0.7 divide_reduce_fusion.1
  338.9 0.1 div.40
  339.0 10.3 %all-to-all-done.5 = f32[16,128,64]{1,2,0:T(8,128)S(1)} async-done(((f32[16,128,64]{1,2,0:T(8,128)}), f32[16,128,64]{1,2,0:T(8,128)S(1)}, u32[]{:S(2)}, u32[]{:S(2)}) %all-to-all-start.5) | async-done | bytes 524320 | tf_op jit(solution)/shard_map/all_to_all | solution.py:97
  349.3 0.2 multiply_add_fusion.1
  349.7 1.9 collective-permute-start.4
  351.6 2.4 collective-permute-start.5
  354.0 0.1 fusion.51
  354.1 1.4 collective-permute-done.4
  355.5 5.9 %collective-permute-done.5 = f32[128,1,4,128]{0,3,2,1:T(8,128)S(1)} collective-permute-done((f32[128,1,4,128]{0,3,2,1:T(8,128)S(1)}, f32[128,1,4,128]{0,3,2,1:T(8,128)S(1)}, u32[]{:S(2)}, u32[]{:S(2)}) %collective-permute-start.5) | collective-permute-done | bytes 262176 | tf_op jit(solution)/shard_map/ppermute | solution.py:16
  361.4 0.3 fusion.42
  361.7 15.9 %all_to_all.130 = bf16[128,16,64]{0,2,1:T(8,128)(2,1)S(1)} all-to-all(bf16[128,16,64]{0,2,1:T(8,128)(2,1)S(1)} %bitcast.99), channel_id=1, replica_groups=mesh['space'=32,'mode'=16] {'mode'}, dimensions={1} | all-to-all | bytes 524288 | tf_op jit(solution)/shard_map/all_to_all | solution.py:92
  377.6 0.3 convolution_bitcast_fusion.3
  377.9 0.6 broadcast_in_dim.60
  378.5 5.3 %all-to-all-start.9 = ((f32[16,1,64]{2,1,0:T(1,128)}), f32[16,1,64]{2,1,0:T(1,128)S(1)}, u32[]{:S(2)}, u32[]{:S(2)}) async-start(f32[16,1,64]{2,1,0:T(1,128)} %broadcast_in_dim.60), calls=%async_computation.9 | async-start | bytes 16384 | tf_op jit(solution)/shard_map/all_to_all | solution.py:27
  383.8 6.0 %convolution_bitcast_fusion = f32[8,16,8,128]{3,2,1,0:T(8,128)S(1)} fusion(bf16[2048,2048]{1,0:T(8,128)(2,1)} %bitcast.5, bf16[128,16,64]{0,2,1:T(8,128)(2,1)S(1)} %all_to_all.130), kind=kOutput, calls=%fused_computation | convolution fusion | flops 536870912 | bytes 9175040 | tf_op jit(solution)/shard_map/dot_general | solution.py:93
  389.8 0.9 copy.60
  390.7 0.8 all-to-all-done.9
  391.5 8.8 %all-to-all-start.8 = ((f32[16,128,64]{1,2,0:T(8,128)}), f32[16,128,64]{1,2,0:T(8,128)S(1)}, u32[]{:S(2)}, u32[]{:S(2)}) async-start(f32[16,128,64]{1,2,0:T(8,128)} %bitcast.93), calls=%async_computation.8 | async-start | bytes 1048576 | tf_op jit(solution)/shard_map/all_to_all | solution.py:97
  400.3 0.7 divide_reduce_fusion
  401.0 0.1 div.42
  401.1 10.1 %all-to-all-done.8 = f32[16,128,64]{1,2,0:T(8,128)S(1)} async-done(((f32[16,128,64]{1,2,0:T(8,128)}), f32[16,128,64]{1,2,0:T(8,128)S(1)}, u32[]{:S(2)}, u32[]{:S(2)}) %all-to-all-start.8) | async-done | bytes 524320 | tf_op jit(solution)/shard_map/all_to_all | solution.py:97
  411.2 0.2 multiply_add_fusion
  411.4 1.0 copy.26
  (19 shorter events, 0.5 us)
Async XLA Ops:
  0.6 41.2 %copy-start = (bf16[128,2048]{1,0:T(8,128)(2,1)S(1)}, bf16[128,2048]{1,0:T(8,128)(2,1)}, u32[]{:S(2)}) copy-start(bf16[128,2048]{1,0:T(8,128)(2,1)} %param.11) | copy-start | bytes 1572868
  3.6 10.5 %collective-permute-start = (f32[128,1,4,128]{0,3,2,1:T(8,128)S(1)}, f32[128,1,4,128]{0,3,2,1:T(8,128)S(1)}, u32[]{:S(2)}, u32[]{:S(2)}) collective-permute-start(f32[128,1,4,128]{0,3,2,1:T(8,128)S(1)} %get-tuple-element.32), channel_id=1, source_target_pairs={{16,0},{32,16},{48,32},{64,48},{80,64},{96,80},{112,96},{128,112},... | collective-permute-start | bytes 786440 | tf_op jit(solution)/shard_map/ppermute | solution.py:18
  10.3 9.8 %collective-permute-start.1 = (f32[128,1,4,128]{0,3,2,1:T(8,128)S(1)}, f32[128,1,4,128]{0,3,2,1:T(8,128)S(1)}, u32[]{:S(2)}, u32[]{:S(2)}) collective-permute-start(f32[128,1,4,128]{0,3,2,1:T(8,128)S(1)} %get-tuple-element.33), channel_id=1, source_target_pairs={{0,16},{16,32},{32,48},{48,64},{64,80},{80,96},{96,112},{112,128},... | collective-permute-start | bytes 786440 | tf_op jit(solution)/shard_map/ppermute | solution.py:16
  46.2 6.5 %copy-start.1 = (f32[2048]{0:T(1024)S(1)}, f32[2048]{0:T(1024)}, u32[]{:S(2)}) copy-start(f32[2048]{0:T(1024)} %param.8) | copy-start | bytes 24580
  46.2 191.3 %all-to-all-start.1 = ((bf16[16,128,2048]{2,1,0:T(8,128)(2,1)}), bf16[16,128,2048]{2,1,0:T(8,128)(2,1)}, u32[]{:S(2)}, u32[]{:S(2)}) async-start(bf16[16,128,2048]{2,1,0:T(8,128)(2,1)} %stack.2), calls=%async_computation.1 | async-start | bytes 16777216 | tf_op jit(solution)/shard_map/all_to_all | solution.py:85
  238.1 14.8 %all-to-all-start.3 = ((f32[16,1,64]{2,1,0:T(1,128)}), f32[16,1,64]{2,1,0:T(1,128)S(1)}, u32[]{:S(2)}, u32[]{:S(2)}) async-start(f32[16,1,64]{2,1,0:T(1,128)} %broadcast_in_dim.58), calls=%async_computation.3 | async-start | bytes 16384 | tf_op jit(solution)/shard_map/all_to_all | solution.py:27
  252.9 20.4 %all-to-all-start.2 = ((f32[16,128,64]{1,2,0:T(8,128)}), f32[16,128,64]{1,2,0:T(8,128)S(1)}, u32[]{:S(2)}, u32[]{:S(2)}) async-start(f32[16,128,64]{1,2,0:T(8,128)} %bitcast.95), calls=%async_computation.2 | async-start | bytes 1048576 | tf_op jit(solution)/shard_map/all_to_all | solution.py:97
  273.8 16.5 %collective-permute-start.2 = (f32[128,1,4,128]{0,3,2,1:T(8,128)S(1)}, f32[128,1,4,128]{0,3,2,1:T(8,128)S(1)}, u32[]{:S(2)}, u32[]{:S(2)}) collective-permute-start(f32[128,1,4,128]{0,3,2,1:T(8,128)S(1)} %get-tuple-element.22), channel_id=1, source_target_pairs={{16,0},{32,16},{48,32},{64,48},{80,64},{96,80},{112,96},{128,112},... | collective-permute-start | bytes 786440 | tf_op jit(solution)/shard_map/ppermute | solution.py:18
  286.3 10.5 %collective-permute-start.3 = (f32[128,1,4,128]{0,3,2,1:T(8,128)S(1)}, f32[128,1,4,128]{0,3,2,1:T(8,128)S(1)}, u32[]{:S(2)}, u32[]{:S(2)}) collective-permute-start(f32[128,1,4,128]{0,3,2,1:T(8,128)S(1)} %get-tuple-element.23), channel_id=1, source_target_pairs={{0,16},{16,32},{32,48},{48,64},{64,80},{80,96},{96,112},{112,128},... | collective-permute-start | bytes 786440 | tf_op jit(solution)/shard_map/ppermute | solution.py:16
  316.5 13.0 %all-to-all-start.6 = ((f32[16,1,64]{2,1,0:T(1,128)}), f32[16,1,64]{2,1,0:T(1,128)S(1)}, u32[]{:S(2)}, u32[]{:S(2)}) async-start(f32[16,1,64]{2,1,0:T(1,128)} %broadcast_in_dim.59), calls=%async_computation.6 | async-start | bytes 16384 | tf_op jit(solution)/shard_map/all_to_all | solution.py:27
  329.5 19.8 %all-to-all-start.5 = ((f32[16,128,64]{1,2,0:T(8,128)}), f32[16,128,64]{1,2,0:T(8,128)S(1)}, u32[]{:S(2)}, u32[]{:S(2)}) async-start(f32[16,128,64]{1,2,0:T(8,128)} %bitcast.94), calls=%async_computation.5 | async-start | bytes 1048576 | tf_op jit(solution)/shard_map/all_to_all | solution.py:97
  349.7 5.8 %collective-permute-start.4 = (f32[128,1,4,128]{0,3,2,1:T(8,128)S(1)}, f32[128,1,4,128]{0,3,2,1:T(8,128)S(1)}, u32[]{:S(2)}, u32[]{:S(2)}) collective-permute-start(f32[128,1,4,128]{0,3,2,1:T(8,128)S(1)} %get-tuple-element.12), channel_id=1, source_target_pairs={{16,0},{32,16},{48,32},{64,48},{80,64},{96,80},{112,96},{128,112},... | collective-permute-start | bytes 786440 | tf_op jit(solution)/shard_map/ppermute | solution.py:18
  351.6 9.8 %collective-permute-start.5 = (f32[128,1,4,128]{0,3,2,1:T(8,128)S(1)}, f32[128,1,4,128]{0,3,2,1:T(8,128)S(1)}, u32[]{:S(2)}, u32[]{:S(2)}) collective-permute-start(f32[128,1,4,128]{0,3,2,1:T(8,128)S(1)} %get-tuple-element.13), channel_id=1, source_target_pairs={{0,16},{16,32},{32,48},{48,64},{64,80},{80,96},{96,112},{112,128},... | collective-permute-start | bytes 786440 | tf_op jit(solution)/shard_map/ppermute | solution.py:16
  378.5 13.0 %all-to-all-start.9 = ((f32[16,1,64]{2,1,0:T(1,128)}), f32[16,1,64]{2,1,0:T(1,128)S(1)}, u32[]{:S(2)}, u32[]{:S(2)}) async-start(f32[16,1,64]{2,1,0:T(1,128)} %broadcast_in_dim.60), calls=%async_computation.9 | async-start | bytes 16384 | tf_op jit(solution)/shard_map/all_to_all | solution.py:27
  391.5 19.7 %all-to-all-start.8 = ((f32[16,128,64]{1,2,0:T(8,128)}), f32[16,128,64]{1,2,0:T(8,128)S(1)}, u32[]{:S(2)}, u32[]{:S(2)}) async-start(f32[16,128,64]{1,2,0:T(8,128)} %bitcast.93), calls=%async_computation.8 | async-start | bytes 1048576 | tf_op jit(solution)/shard_map/all_to_all | solution.py:97
  401.1 11.4 %copy-start.2 = (f32[2,4,128]{2,1,0:T(4,128)}, f32[2,4,128]{2,1,0:T(4,128)S(1)}, u32[]{:S(2)}) copy-start(f32[2,4,128]{2,1,0:T(4,128)S(1)} %div.42) | copy-start | bytes 12292
